TPU v7x, 512 devices: a whole 4x8x8 slice. The times are simulated.
512 devices in a mesh: loop: 16 (over y, x_hi), dp: 32 (over z, x_lo, core).
Axes of the slice: x: 4 (x_hi: 2, x_lo: 2; x = x_hi * 2 + x_lo), y: 8, z: 8, core: 2. Of those that a mesh axis runs over, the one named last changes fastest.
Arguments:
- images: bfloat16 [32, 32, 16, 16, 768], P('dp', 'loop'), may hold values from -6 to 6
- kernel: float32 [7, 7, 768], replicated, may hold values from -0.875 to 0.875
- ln_gain: float32 [768], replicated, may hold values from 0.5 to 1.5
- w_up: bfloat16 [768, 1536], P('dp'), may hold values from -0.21875 to 0.21875
- b_up: float32 [1536], replicated, may hold values from -3 to 3
- w_down: bfloat16 [1536, 768], P('dp'), may hold values from -0.15625 to 0.15625
- layer_scale: float32 [768], replicated, may hold values from 0.3 to 1
- w_head: bfloat16 [768, 1152], P('dp'), may hold values from -0.21875 to 0.21875
- text_rows: bfloat16 [32, 32, 1152], P('dp', 'loop'), may hold values from -6 to 6
- pair_ids: int32 [32, 32], P('dp', 'loop'), may hold values from 0 to 31, each once within a row
- log_temp: float32 [1], replicated, may hold values from 1.5 to 2.5
- loss_bias: float32 [1], replicated, may hold values from -6 to -2
Outputs:
- kernel_grad: float32 [7, 7, 768], replicated
- up_grad: float32 [768, 1536], P('dp')
- text_grad: float32 [32, 32, 1152], P('dp', 'loop')
Inputs may be any that keep to these rules, and one draw needn't show every extreme that they name: Each row of pair_ids holds every index of its group once.
All inputs are finite; a program needn't handle non-finite values.
Results may differ from a plain program's by a relative error of at most 0.04.
Values may be sent and summed in bfloat16 or wider, within the bound.
A program may use at most 64 MiB of HBM per device.

v0:
```python
import jax
import jax.numpy as jnp
from jax import lax
from jax.sharding import PartitionSpec as P

epsilon = 1e-06


def passed_along(value, axis, steps):
    count = lax.axis_size(axis)
    pairs = [(source, (source + steps) % count) for source in range(count)]
    return lax.ppermute(value, axis, pairs)


def image_tower(kernel, w_up, images, ln_gain, b_up, w_down, layer_scale, w_head):
    image_count = images.shape[0]
    grid_side = images.shape[1]
    channels = images.shape[3]
    padded = jnp.pad(images, ((0, 0), (3, 3), (3, 3), (0, 0)))
    conv_out = jnp.zeros(images.shape, jnp.float32)
    for row_off in range(7):
        for col_off in range(7):
            window = padded[:, row_off : row_off + grid_side, col_off : col_off + grid_side, :]
            conv_out = conv_out + window.astype(jnp.float32) * kernel[row_off, col_off]
    chan_mean = jnp.mean(conv_out, axis=-1, keepdims=True)
    centered = conv_out - chan_mean
    chan_var = jnp.mean(centered * centered, axis=-1, keepdims=True)
    normed = (centered * lax.rsqrt(chan_var + epsilon) * ln_gain).astype(jnp.bfloat16)
    flat_rows = normed.reshape(-1, channels)
    hidden = jnp.dot(flat_rows, w_up, preferred_element_type=jnp.float32) + b_up
    active = jax.nn.gelu(hidden, approximate=True).astype(jnp.bfloat16)
    mlp_out = jnp.dot(active, w_down, preferred_element_type=jnp.float32)
    block_out = images.reshape(-1, channels).astype(jnp.float32) + layer_scale * mlp_out
    pooled = jnp.mean(
        block_out.reshape(image_count, grid_side * grid_side, channels), axis=1
    ).astype(jnp.bfloat16)
    embedding = jnp.dot(pooled, w_head, preferred_element_type=jnp.float32)
    return embedding * lax.rsqrt(jnp.sum(embedding * embedding, axis=-1, keepdims=True) + epsilon)


def pair_grad(image_emb, text_emb, pair_row, text_index, logit_scale, logit_bias, group_size):
    logits = (
        logit_scale * jnp.dot(image_emb, text_emb.T, precision=lax.Precision.HIGHEST) + logit_bias
    )
    sign_of = jnp.where(pair_row[:, None] == text_index[None, :], 1.0, -1.0)
    return -sign_of * jax.nn.sigmoid(-sign_of * logits) / group_size


def body(
    images,
    kernel,
    ln_gain,
    w_up,
    b_up,
    w_down,
    layer_scale,
    w_head,
    text_rows,
    pair_ids,
    log_temp,
    loss_bias,
):
    loop_size = lax.axis_size("loop")
    loop_index = lax.axis_index("loop")
    up_full, down_full, head_full = (
        lax.all_gather(w_up, "dp", axis=0, tiled=True),
        lax.all_gather(w_down, "dp", axis=0, tiled=True),
        lax.all_gather(w_head, "dp", axis=0, tiled=True),
    )
    pictures = images[0]
    pair_row = pair_ids[0]
    img_dev = pictures.shape[0]
    group_size = img_dev * loop_size
    logit_scale = jnp.exp(log_temp[0])
    logit_bias = loss_bias[0]

    def run_tower(kernel_arg, up_arg):
        return image_tower(
            kernel_arg, up_arg, pictures, ln_gain, b_up, down_full, layer_scale, head_full
        )

    image_emb, pullback = jax.vjp(run_tower, kernel, up_full)
    raw_rows = text_rows[0].astype(jnp.float32)
    text_norm = jnp.sqrt(jnp.sum(raw_rows * raw_rows, axis=-1, keepdims=True) + epsilon)
    text_hat = raw_rows / text_norm
    rounded = lax.optimization_barrier(text_hat.astype(jnp.bfloat16))
    local_index = jnp.arange(img_dev, dtype=jnp.int32)

    def cycle_step(step_index, state):
        text_block, partials, image_cot = state
        source = (loop_index - step_index) % loop_size
        text_index = source * img_dev + local_index
        pair_weight = pair_grad(
            image_emb, text_block, pair_row, text_index, logit_scale, logit_bias, group_size
        )
        image_cot = image_cot + logit_scale * jnp.dot(
            pair_weight, text_block, precision=lax.Precision.HIGHEST
        )
        partials = partials + logit_scale * jnp.dot(
            pair_weight.T, image_emb, precision=lax.Precision.HIGHEST
        )
        text_block, partials = passed_along((text_block, partials), "loop", 1)
        return (text_block, partials, image_cot)

    start = (
        rounded.astype(jnp.float32),
        jnp.zeros(raw_rows.shape, jnp.float32),
        jnp.zeros(image_emb.shape, jnp.float32),
    )
    _, text_cot, image_cot = lax.fori_loop(0, loop_size, cycle_step, start)
    text_grad = (
        text_cot - text_hat * jnp.sum(text_hat * text_cot, axis=-1, keepdims=True)
    ) / text_norm
    kernel_part, up_part = pullback(image_cot)
    kernel_grad = lax.psum(kernel_part, ("loop", "dp"))
    up_rows = lax.psum_scatter(
        up_part.astype(jnp.float32).astype(jnp.bfloat16), "dp", scatter_dimension=0, tiled=True
    )
    up_grad = lax.psum(up_rows, "loop").astype(jnp.float32)
    return (kernel_grad, up_grad, text_grad[None])


def solution(mesh):
    placed = (
        P("dp", "loop", None, None, None),
        P(),
        P(),
        P("dp", None),
        P(),
        P("dp", None),
        P(),
        P("dp", None),
        P("dp", "loop", None),
        P("dp", "loop"),
        P(),
        P(),
    )
    return jax.shard_map(
        body,
        mesh=mesh,
        in_specs=placed,
        out_specs=(P(), P("dp", None), P("dp", "loop", None)),
        check_vma=False,
    )
```

profile of v0, /device:TPU:1, one launch (start us, length us, event | category | flops | bytes accessed | tf_op | source)
XLA Modules:
  0.0 996.5 jit_solution(3485320233537033907)
XLA Ops:
  15.5 30.5 %fusion.140 = (f32[2,16,16]{2,1,0:T(8,128)S(1)}, f32[2,16,16,768]{3,2,1,0:T(8,128)S(1)}) fusion(f32[768]{0:T(1024)S(1)} %get-tuple-element.377, f32[768]{0:T(1024)S(1)} %get-tuple-element.378, f32[768]{0:T(1024)S(1)} %get-tuple-element.331, f32[768]{0:T(1024)S(1)} %get-tuple-element.332, f32[768]{0:T(1024)S(1)} %get-tuple-element.333, ...), kind=kLoop, calls=%fused_computation.374 | loop fusion | flops 57802240 | bytes 2511872 | tf_op jit(solution)/shard_map/jvp()/reduce_sum | solution.py:25
  46.7 37.7 %all-gather.4.cloned.1.call-done = bf16[768,1536]{1,0:T(8,128)(2,1)} async-done(((bf16[24,1536]{1,0:T(8,128)(2,1)}), bf16[768,1536]{1,0:T(8,128)(2,1)}) %all-gather.4.cloned.1.call-update) | async-done | bytes 2359312 | tf_op jit(solution)/shard_map/all_gather | solution.py:66
  84.4 4.8 convolution_add_fusion
  89.2 65.1 %all-gather.6.cloned.1.call-done = bf16[1536,768]{1,0:T(8,128)(2,1)} async-done(((bf16[48,768]{1,0:T(8,128)(2,1)}), bf16[1536,768]{1,0:T(8,128)(2,1)}) %all-gather.6.cloned.1.call-update) | async-done | bytes 2359312 | tf_op jit(solution)/shard_map/all_gather | solution.py:67
  154.3 4.6 bitcast_reduce_fusion
  158.9 64.5 %all-gather.8.cloned.1.call-done = bf16[768,1152]{1,0:T(8,128)(2,1)} async-done(((bf16[24,1152]{1,0:T(8,128)(2,1)}), bf16[768,1152]{1,0:T(8,128)(2,1)}) %all-gather.8.cloned.1.call-update) | async-done | bytes 1769488 | tf_op jit(solution)/shard_map/all_gather | solution.py:68
  225.4 184.7 %while.20 = (s32[]{:T(128)}, f32[2,1152]{1,0:T(2,128)S(1)}, f32[2,1152]{1,0:T(2,128)S(1)}, f32[2,1152]{1,0:T(2,128)S(1)}, f32[]{:T(128)}, /*index=5*/s32[1,2]{1,...) while((s32[]{:T(128)}, f32[2,1152]{1,0:T(2,128)S(1)}, ...), condition=%wide.region_6.7_spmd.clone, body=%wide.region_5.6_spmd.clone.sunk | while | flops 177470 | bytes 166336 | solution.py:110
  225.5 4.3 collective-permute-start
  234.5 4.4 collective-permute-done.1
  242.0 4.6 collective-permute-start.1
  257.3 4.4 collective-permute-done.1
  264.8 4.6 collective-permute-start.1
  280.0 4.4 collective-permute-done.1
  287.5 4.6 collective-permute-start.1
  299.1 5.2 collective-permute-start.1
  311.4 6.0 collective-permute-start.1
  361.8 4.1 collective-permute-done.1
  372.8 4.1 collective-permute-done.1
  402.2 4.1 collective-permute-start.1
  412.6 4.6 fusion.14
  426.0 5.0 fusion.117
  440.1 119.1 %reduce-scatter.2.cloned.1.call-done = bf16[24,1536]{1,0:T(8,128)(2,1)} async-done(((bf16[768,1536]{1,0:T(8,128)(2,1)}), bf16[24,1536]{1,0:T(8,128)(2,1)}) %reduce-scatter.2.cloned.1.call-update) | async-done | bytes 73744 | tf_op jit(solution)/shard_map/reduce_scatter | solution.py:116
  560.5 148.9 %all-reduce.55.cloned.1.call-done = bf16[24,1536]{1,0:T(8,128)(2,1)} async-done(((bf16[24,1536]{1,0:T(8,128)(2,1)}), bf16[24,1536]{1,0:T(8,128)(2,1)}) %all-reduce.55.cloned.1.call-update) | async-done | bytes 73744 | tf_op jit(solution)/shard_map/psum | solution.py:119
  711.0 277.1 %all-reduce.53.cloned.1.call-done = f32[7,7,768]{2,1,0:T(8,128)} async-done(((f32[7,7,768]{2,1,0:T(8,128)}), f32[7,7,768]{2,1,0:T(8,128)}) %all-reduce.53.cloned.1.call-update) | async-done | bytes 150544 | tf_op jit(solution)/shard_map/psum | solution.py:115
  (240 shorter events, 163.2 us)
Async XLA Ops:
  7.2 77.2 %all-gather.4.cloned.1.call-start = ((), (), s32[]{:S(2)}) async-start(), calls=%async_computation.1 | async-start | bytes 2433024 | tf_op jit(solution)/shard_map/all_gather | solution.py:66
  7.9 146.4 %all-gather.6.cloned.1.call-start = ((), (), s32[]{:S(2)}) async-start(), calls=%async_computation.2 | async-start | bytes 2433024 | tf_op jit(solution)/shard_map/all_gather | solution.py:67
  8.6 214.8 %all-gather.8.cloned.1.call-start = ((), (), s32[]{:S(2)}) async-start(), calls=%async_computation.3 | async-start | bytes 1824768 | tf_op jit(solution)/shard_map/all_gather | solution.py:68
  9.4 549.9 %reduce-scatter.2.cloned.1.call-start = ((), (), s32[]{:S(2)}) async-start(), calls=%async_computation.5 | async-start | bytes 2433024 | tf_op jit(solution)/shard_map/reduce_scatter | solution.py:116
  225.5 13.5 %collective-permute-start = (f32[2,1152]{1,0:T(2,128)S(1)}, f32[2,1152]{1,0:T(2,128)S(1)}, u32[]{:S(2)}, u32[]{:S(2)}) collective-permute-start(f32[2,1152]{1,0:T(2,128)S(1)} %copy.20), channel_id=1, source_target_pairs={{0,32},{32,64},{64,96},{96,128},{128,160},{160,192},{192,224},{224... | collective-permute-start | bytes 27656 | tf_op jit(solution)/shard_map/while/body/eval_jaxpr/ppermute | solution.py:12
  239.0 11.1 %collective-permute-start = (f32[2,1152]{1,0:T(2,128)S(1)}, f32[2,1152]{1,0:T(2,128)S(1)}, u32[]{:S(2)}, u32[]{:S(2)}) collective-permute-start(f32[2,1152]{1,0:T(2,128)S(1)} %copy.20), channel_id=1, source_target_pairs={{0,32},{32,64},{64,96},{96,128},{128,160},{160,192},{192,224},{224... | collective-permute-start | bytes 27656 | tf_op jit(solution)/shard_map/while/body/eval_jaxpr/ppermute | solution.py:12
  250.1 11.6 %collective-permute-start = (f32[2,1152]{1,0:T(2,128)S(1)}, f32[2,1152]{1,0:T(2,128)S(1)}, u32[]{:S(2)}, u32[]{:S(2)}) collective-permute-start(f32[2,1152]{1,0:T(2,128)S(1)} %copy.20), channel_id=1, source_target_pairs={{0,32},{32,64},{64,96},{96,128},{128,160},{160,192},{192,224},{224... | collective-permute-start | bytes 27656 | tf_op jit(solution)/shard_map/while/body/eval_jaxpr/ppermute | solution.py:12
  261.7 11.1 %collective-permute-start = (f32[2,1152]{1,0:T(2,128)S(1)}, f32[2,1152]{1,0:T(2,128)S(1)}, u32[]{:S(2)}, u32[]{:S(2)}) collective-permute-start(f32[2,1152]{1,0:T(2,128)S(1)} %copy.20), channel_id=1, source_target_pairs={{0,32},{32,64},{64,96},{96,128},{128,160},{160,192},{192,224},{224... | collective-permute-start | bytes 27656 | tf_op jit(solution)/shard_map/while/body/eval_jaxpr/ppermute | solution.py:12
  272.8 11.6 %collective-permute-start = (f32[2,1152]{1,0:T(2,128)S(1)}, f32[2,1152]{1,0:T(2,128)S(1)}, u32[]{:S(2)}, u32[]{:S(2)}) collective-permute-start(f32[2,1152]{1,0:T(2,128)S(1)} %copy.20), channel_id=1, source_target_pairs={{0,32},{32,64},{64,96},{96,128},{128,160},{160,192},{192,224},{224... | collective-permute-start | bytes 27656 | tf_op jit(solution)/shard_map/while/body/eval_jaxpr/ppermute | solution.py:12
  284.4 11.1 %collective-permute-start = (f32[2,1152]{1,0:T(2,128)S(1)}, f32[2,1152]{1,0:T(2,128)S(1)}, u32[]{:S(2)}, u32[]{:S(2)}) collective-permute-start(f32[2,1152]{1,0:T(2,128)S(1)} %copy.20), channel_id=1, source_target_pairs={{0,32},{32,64},{64,96},{96,128},{128,160},{160,192},{192,224},{224... | collective-permute-start | bytes 27656 | tf_op jit(solution)/shard_map/while/body/eval_jaxpr/ppermute | solution.py:12
  295.5 11.6 %collective-permute-start = (f32[2,1152]{1,0:T(2,128)S(1)}, f32[2,1152]{1,0:T(2,128)S(1)}, u32[]{:S(2)}, u32[]{:S(2)}) collective-permute-start(f32[2,1152]{1,0:T(2,128)S(1)} %copy.20), channel_id=1, source_target_pairs={{0,32},{32,64},{64,96},{96,128},{128,160},{160,192},{192,224},{224... | collective-permute-start | bytes 27656 | tf_op jit(solution)/shard_map/while/body/eval_jaxpr/ppermute | solution.py:12
  307.1 12.3 %collective-permute-start = (f32[2,1152]{1,0:T(2,128)S(1)}, f32[2,1152]{1,0:T(2,128)S(1)}, u32[]{:S(2)}, u32[]{:S(2)}) collective-permute-start(f32[2,1152]{1,0:T(2,128)S(1)} %copy.20), channel_id=1, source_target_pairs={{0,32},{32,64},{64,96},{96,128},{128,160},{160,192},{192,224},{224... | collective-permute-start | bytes 27656 | tf_op jit(solution)/shard_map/while/body/eval_jaxpr/ppermute | solution.py:12
  319.4 13.1 %collective-permute-start = (f32[2,1152]{1,0:T(2,128)S(1)}, f32[2,1152]{1,0:T(2,128)S(1)}, u32[]{:S(2)}, u32[]{:S(2)}) collective-permute-start(f32[2,1152]{1,0:T(2,128)S(1)} %copy.20), channel_id=1, source_target_pairs={{0,32},{32,64},{64,96},{96,128},{128,160},{160,192},{192,224},{224... | collective-permute-start | bytes 27656 | tf_op jit(solution)/shard_map/while/body/eval_jaxpr/ppermute | solution.py:12
  332.5 11.2 %collective-permute-start = (f32[2,1152]{1,0:T(2,128)S(1)}, f32[2,1152]{1,0:T(2,128)S(1)}, u32[]{:S(2)}, u32[]{:S(2)}) collective-permute-start(f32[2,1152]{1,0:T(2,128)S(1)} %copy.20), channel_id=1, source_target_pairs={{0,32},{32,64},{64,96},{96,128},{128,160},{160,192},{192,224},{224... | collective-permute-start | bytes 27656 | tf_op jit(solution)/shard_map/while/body/eval_jaxpr/ppermute | solution.py:12
  343.7 11.1 %collective-permute-start = (f32[2,1152]{1,0:T(2,128)S(1)}, f32[2,1152]{1,0:T(2,128)S(1)}, u32[]{:S(2)}, u32[]{:S(2)}) collective-permute-start(f32[2,1152]{1,0:T(2,128)S(1)} %copy.20), channel_id=1, source_target_pairs={{0,32},{32,64},{64,96},{96,128},{128,160},{160,192},{192,224},{224... | collective-permute-start | bytes 27656 | tf_op jit(solution)/shard_map/while/body/eval_jaxpr/ppermute | solution.py:12
  354.7 11.1 %collective-permute-start = (f32[2,1152]{1,0:T(2,128)S(1)}, f32[2,1152]{1,0:T(2,128)S(1)}, u32[]{:S(2)}, u32[]{:S(2)}) collective-permute-start(f32[2,1152]{1,0:T(2,128)S(1)} %copy.20), channel_id=1, source_target_pairs={{0,32},{32,64},{64,96},{96,128},{128,160},{160,192},{192,224},{224... | collective-permute-start | bytes 27656 | tf_op jit(solution)/shard_map/while/body/eval_jaxpr/ppermute | solution.py:12
  365.8 11.1 %collective-permute-start = (f32[2,1152]{1,0:T(2,128)S(1)}, f32[2,1152]{1,0:T(2,128)S(1)}, u32[]{:S(2)}, u32[]{:S(2)}) collective-permute-start(f32[2,1152]{1,0:T(2,128)S(1)} %copy.20), channel_id=1, source_target_pairs={{0,32},{32,64},{64,96},{96,128},{128,160},{160,192},{192,224},{224... | collective-permute-start | bytes 27656 | tf_op jit(solution)/shard_map/while/body/eval_jaxpr/ppermute | solution.py:12
  368.9 8.0 collective-permute-start.1
  376.9 11.1 %collective-permute-start = (f32[2,1152]{1,0:T(2,128)S(1)}, f32[2,1152]{1,0:T(2,128)S(1)}, u32[]{:S(2)}, u32[]{:S(2)}) collective-permute-start(f32[2,1152]{1,0:T(2,128)S(1)} %copy.20), channel_id=1, source_target_pairs={{0,32},{32,64},{64,96},{96,128},{128,160},{160,192},{192,224},{224... | collective-permute-start | bytes 27656 | tf_op jit(solution)/shard_map/while/body/eval_jaxpr/ppermute | solution.py:12
  380.0 8.0 collective-permute-start.1
  388.0 11.1 %collective-permute-start = (f32[2,1152]{1,0:T(2,128)S(1)}, f32[2,1152]{1,0:T(2,128)S(1)}, u32[]{:S(2)}, u32[]{:S(2)}) collective-permute-start(f32[2,1152]{1,0:T(2,128)S(1)} %copy.20), channel_id=1, source_target_pairs={{0,32},{32,64},{64,96},{96,128},{128,160},{160,192},{192,224},{224... | collective-permute-start | bytes 27656 | tf_op jit(solution)/shard_map/while/body/eval_jaxpr/ppermute | solution.py:12
  399.1 11.1 %collective-permute-start = (f32[2,1152]{1,0:T(2,128)S(1)}, f32[2,1152]{1,0:T(2,128)S(1)}, u32[]{:S(2)}, u32[]{:S(2)}) collective-permute-start(f32[2,1152]{1,0:T(2,128)S(1)} %copy.20), channel_id=1, source_target_pairs={{0,32},{32,64},{64,96},{96,128},{128,160},{160,192},{192,224},{224... | collective-permute-start | bytes 27656 | tf_op jit(solution)/shard_map/while/body/eval_jaxpr/ppermute | solution.py:12
  421.2 288.2 %all-reduce.55.cloned.1.call-start = ((), (), s32[]{:S(2)}) async-start(), calls=%async_computation.6 | async-start | bytes 147456 | tf_op jit(solution)/shard_map/psum | solution.py:119
  559.3 428.8 %all-reduce.53.cloned.1.call-start = ((), (), s32[]{:S(2)}) async-start(), calls=%async_computation.4 | async-start | bytes 344064 | tf_op jit(solution)/shard_map/psum | solution.py:115
  (21 other events, 391.1 us)
Sparse Core Ops, SparseCore 0:
  10.1 74.2 all-gather.3
  86.5 67.7 all-gather.5
  156.5 66.9 all-gather.7
  421.4 137.8 reduce-scatter.1
  562.0 147.3 all-reduce.54
  715.6 272.4 all-reduce.52
where the time goes:
time: 998 us; the launch traced here: 997 us
  waiting for transfers between devices  774 us (78%)
  starting transfers between devices  104 us (10%)
  other arithmetic  50 us (5%)
  matrix products  44.9 us (4%)
  between operations  15.4 us (2%)
    psum x1, waiting for transfers between devices, body(): kernel_grad = lax.psum(kernel_part, ('loop', 'dp'))  277 us
    psum x1, waiting for transfers between devices, body(): up_grad = lax.psum(up_rows, 'loop').astype(jnp.float32)  149 us
    reduce_scatter x1, waiting for transfers between devices, body(): lax.psum_scatter(up_part.astype(jnp.float32).astype(jnp.bfloat16), 'dp',...  119 us
    ppermute x32, starting transfers between devices, passed_along(): return lax.ppermute(value, axis, pairs)  104 us
    all_gather x1, waiting for transfers between devices, body(): lax.all_gather(w_down, 'dp', axis=0, tiled=True)  65.1 us
    all_gather x1, waiting for transfers between devices, body(): lax.all_gather(w_head, 'dp', axis=0, tiled=True)  64.5 us
    ppermute x32, waiting for transfers between devices, passed_along(): return lax.ppermute(value, axis, pairs)  59.5 us
    all_gather x1, waiting for transfers between devices, body(): lax.all_gather(w_up, 'dp', axis=0, tiled=True)  37.7 us
  transfers between devices with their start and end apart: 38, of which 22 were waited for; matrix products, arithmetic and copies ran while one was open for 9% of the time, Pallas kernels for 0%

commit v1 on v0

--- a/solution.py
+++ b/solution.py
@@ -112,7 +112,7 @@
         text_cot - text_hat * jnp.sum(text_hat * text_cot, axis=-1, keepdims=True)
     ) / text_norm
     kernel_part, up_part = pullback(image_cot)
-    kernel_grad = lax.psum(kernel_part, ("loop", "dp"))
+    kernel_grad = lax.psum(lax.psum(kernel_part, axis_name="dp"), axis_name="loop")
     up_rows = lax.psum_scatter(
         up_part.astype(jnp.float32).astype(jnp.bfloat16), "dp", scatter_dimension=0, tiled=True
     )

time: 998 us -> 1110 us (1.11)
  waiting for transfers between devices: 774 us -> 876 us
    psum x1 -> x2, waiting for transfers between devices: 277 us -> 378 us  [the longest x1 217 us: body(): lax.psum(kernel_part, axis_name='dp')]
  transfers between devices with their start and end apart: 38 -> 39, of which waited for: 22 -> 23; matrix products, arithmetic and copies ran while one was open for 9% -> 8% of each run, Pallas kernels for 0% -> 0%
where the time goes in v1:
time: 1110 us; the launch traced here: 1100 us
  waiting for transfers between devices  876 us (79%)
  starting transfers between devices  104 us (9%)
  other arithmetic  50.4 us (5%)
  matrix products  45 us (4%)
  between operations  15.4 us (1%)
    psum x1, waiting for transfers between devices, body(): lax.psum(kernel_part, axis_name='dp')  217 us
    psum x1, waiting for transfers between devices, body(): lax.psum(lax.psum(kernel_part, axis_name='dp'), axis_name='loop')  161 us
    psum x1, waiting for transfers between devices, body(): up_grad = lax.psum(up_rows, 'loop').astype(jnp.float32)  151 us
    reduce_scatter x1, waiting for transfers between devices, body(): lax.psum_scatter(up_part.astype(jnp.float32).astype(jnp.bfloat16), 'dp',...  119 us
    ppermute x32, starting transfers between devices, passed_along(): return lax.ppermute(value, axis, pairs)  104 us
    all_gather x1, waiting for transfers between devices, body(): lax.all_gather(w_down, 'dp', axis=0, tiled=True)  65.1 us
    all_gather x1, waiting for transfers between devices, body(): lax.all_gather(w_head, 'dp', axis=0, tiled=True)  64.5 us
    ppermute x32, waiting for transfers between devices, passed_along(): return lax.ppermute(value, axis, pairs)  59.3 us
  transfers between devices with their start and end apart: 39, of which 23 were waited for; matrix products, arithmetic and copies ran while one was open for 8% of the time, Pallas kernels for 0%

profile of v1, /device:TPU:1, one launch (start us, length us, event | category | flops | bytes accessed | tf_op | source)
XLA Modules:
  0.0 1099.2 jit_solution(10667623232011399382)
XLA Ops:
  15.5 30.9 %fusion.140 = (f32[2,16,16]{2,1,0:T(8,128)S(1)}, f32[2,16,16,768]{3,2,1,0:T(8,128)S(1)}) fusion(f32[768]{0:T(1024)S(1)} %get-tuple-element.377, f32[768]{0:T(1024)S(1)} %get-tuple-element.378, f32[768]{0:T(1024)S(1)} %get-tuple-element.331, f32[768]{0:T(1024)S(1)} %get-tuple-element.332, f32[768]{0:T(1024)S(1)} %get-tuple-element.333, ...), kind=kLoop, calls=%fused_computation.374 | loop fusion | flops 57802240 | bytes 2511872 | tf_op jit(solution)/shard_map/jvp()/reduce_sum | solution.py:25
  47.0 37.4 %all-gather.4.cloned.1.call-done = bf16[768,1536]{1,0:T(8,128)(2,1)} async-done(((bf16[24,1536]{1,0:T(8,128)(2,1)}), bf16[768,1536]{1,0:T(8,128)(2,1)}) %all-gather.4.cloned.1.call-update) | async-done | bytes 2359312 | tf_op jit(solution)/shard_map/all_gather | solution.py:66
  84.4 4.8 convolution_add_fusion
  89.2 65.1 %all-gather.6.cloned.1.call-done = bf16[1536,768]{1,0:T(8,128)(2,1)} async-done(((bf16[48,768]{1,0:T(8,128)(2,1)}), bf16[1536,768]{1,0:T(8,128)(2,1)}) %all-gather.6.cloned.1.call-update) | async-done | bytes 2359312 | tf_op jit(solution)/shard_map/all_gather | solution.py:67
  154.3 4.6 bitcast_reduce_fusion
  158.9 64.5 %all-gather.8.cloned.1.call-done = bf16[768,1152]{1,0:T(8,128)(2,1)} async-done(((bf16[24,1152]{1,0:T(8,128)(2,1)}), bf16[768,1152]{1,0:T(8,128)(2,1)}) %all-gather.8.cloned.1.call-update) | async-done | bytes 1769488 | tf_op jit(solution)/shard_map/all_gather | solution.py:68
  225.5 184.7 %while.20 = (s32[]{:T(128)}, f32[2,1152]{1,0:T(2,128)S(1)}, f32[2,1152]{1,0:T(2,128)S(1)}, f32[2,1152]{1,0:T(2,128)S(1)}, f32[]{:T(128)}, /*index=5*/s32[1,2]{1,...) while((s32[]{:T(128)}, f32[2,1152]{1,0:T(2,128)S(1)}, ...), condition=%wide.region_6.7_spmd.clone, body=%wide.region_5.6_spmd.clone.sunk | while | flops 177470 | bytes 166336 | solution.py:110
  225.5 4.3 collective-permute-start
  234.6 4.4 collective-permute-done.1
  242.1 4.6 collective-permute-start.1
  257.3 4.4 collective-permute-done.1
  264.8 4.6 collective-permute-start.1
  280.0 4.4 collective-permute-done.1
  287.5 4.6 collective-permute-start.1
  299.1 5.2 collective-permute-start.1
  311.4 6.0 collective-permute-start.1
  361.8 4.1 collective-permute-done.1
  402.2 4.1 collective-permute-start.1
  412.6 4.6 fusion.14
  426.0 5.0 fusion.117
  440.2 119.0 %reduce-scatter.2.cloned.1.call-done = bf16[24,1536]{1,0:T(8,128)(2,1)} async-done(((bf16[768,1536]{1,0:T(8,128)(2,1)}), bf16[24,1536]{1,0:T(8,128)(2,1)}) %reduce-scatter.2.cloned.1.call-update) | async-done | bytes 73744 | tf_op jit(solution)/shard_map/reduce_scatter | solution.py:116
  559.4 217.3 %all-reduce.54.cloned.1.call-done = f32[7,7,768]{2,1,0:T(8,128)} async-done(((f32[7,7,768]{2,1,0:T(8,128)}), f32[7,7,768]{2,1,0:T(8,128)}) %all-reduce.54.cloned.1.call-update) | async-done | bytes 150544 | tf_op jit(solution)/shard_map/psum | solution.py:115
  777.5 150.7 %all-reduce.58.cloned.1.call-done = bf16[24,1536]{1,0:T(8,128)(2,1)} async-done(((bf16[24,1536]{1,0:T(8,128)(2,1)}), bf16[24,1536]{1,0:T(8,128)(2,1)}) %all-reduce.58.cloned.1.call-update) | async-done | bytes 73744 | tf_op jit(solution)/shard_map/psum | solution.py:119
  929.7 161.0 %all-reduce.56.cloned.1.call-done = f32[7,7,768]{2,1,0:T(8,128)} async-done(((f32[7,7,768]{2,1,0:T(8,128)}), f32[7,7,768]{2,1,0:T(8,128)}) %all-reduce.56.cloned.1.call-update) | async-done | bytes 150544 | tf_op jit(solution)/shard_map/psum | solution.py:115
  (243 shorter events, 166.9 us)
Async XLA Ops:
  7.2 77.2 %all-gather.4.cloned.1.call-start = ((), (), s32[]{:S(2)}) async-start(), calls=%async_computation.1 | async-start | bytes 2433024 | tf_op jit(solution)/shard_map/all_gather | solution.py:66
  7.9 146.4 %all-gather.6.cloned.1.call-start = ((), (), s32[]{:S(2)}) async-start(), calls=%async_computation.2 | async-start | bytes 2433024 | tf_op jit(solution)/shard_map/all_gather | solution.py:67
  8.6 214.8 %all-gather.8.cloned.1.call-start = ((), (), s32[]{:S(2)}) async-start(), calls=%async_computation.3 | async-start | bytes 1824768 | tf_op jit(solution)/shard_map/all_gather | solution.py:68
  9.4 549.9 %reduce-scatter.2.cloned.1.call-start = ((), (), s32[]{:S(2)}) async-start(), calls=%async_computation.6 | async-start | bytes 2433024 | tf_op jit(solution)/shard_map/reduce_scatter | solution.py:116
  225.5 13.5 %collective-permute-start = (f32[2,1152]{1,0:T(2,128)S(1)}, f32[2,1152]{1,0:T(2,128)S(1)}, u32[]{:S(2)}, u32[]{:S(2)}) collective-permute-start(f32[2,1152]{1,0:T(2,128)S(1)} %copy.20), channel_id=1, source_target_pairs={{0,32},{32,64},{64,96},{96,128},{128,160},{160,192},{192,224},{224... | collective-permute-start | bytes 27656 | tf_op jit(solution)/shard_map/while/body/eval_jaxpr/ppermute | solution.py:12
  239.0 11.1 %collective-permute-start = (f32[2,1152]{1,0:T(2,128)S(1)}, f32[2,1152]{1,0:T(2,128)S(1)}, u32[]{:S(2)}, u32[]{:S(2)}) collective-permute-start(f32[2,1152]{1,0:T(2,128)S(1)} %copy.20), channel_id=1, source_target_pairs={{0,32},{32,64},{64,96},{96,128},{128,160},{160,192},{192,224},{224... | collective-permute-start | bytes 27656 | tf_op jit(solution)/shard_map/while/body/eval_jaxpr/ppermute | solution.py:12
  250.1 11.6 %collective-permute-start = (f32[2,1152]{1,0:T(2,128)S(1)}, f32[2,1152]{1,0:T(2,128)S(1)}, u32[]{:S(2)}, u32[]{:S(2)}) collective-permute-start(f32[2,1152]{1,0:T(2,128)S(1)} %copy.20), channel_id=1, source_target_pairs={{0,32},{32,64},{64,96},{96,128},{128,160},{160,192},{192,224},{224... | collective-permute-start | bytes 27656 | tf_op jit(solution)/shard_map/while/body/eval_jaxpr/ppermute | solution.py:12
  261.7 11.1 %collective-permute-start = (f32[2,1152]{1,0:T(2,128)S(1)}, f32[2,1152]{1,0:T(2,128)S(1)}, u32[]{:S(2)}, u32[]{:S(2)}) collective-permute-start(f32[2,1152]{1,0:T(2,128)S(1)} %copy.20), channel_id=1, source_target_pairs={{0,32},{32,64},{64,96},{96,128},{128,160},{160,192},{192,224},{224... | collective-permute-start | bytes 27656 | tf_op jit(solution)/shard_map/while/body/eval_jaxpr/ppermute | solution.py:12
  272.8 11.6 %collective-permute-start = (f32[2,1152]{1,0:T(2,128)S(1)}, f32[2,1152]{1,0:T(2,128)S(1)}, u32[]{:S(2)}, u32[]{:S(2)}) collective-permute-start(f32[2,1152]{1,0:T(2,128)S(1)} %copy.20), channel_id=1, source_target_pairs={{0,32},{32,64},{64,96},{96,128},{128,160},{160,192},{192,224},{224... | collective-permute-start | bytes 27656 | tf_op jit(solution)/shard_map/while/body/eval_jaxpr/ppermute | solution.py:12
  284.4 11.1 %collective-permute-start = (f32[2,1152]{1,0:T(2,128)S(1)}, f32[2,1152]{1,0:T(2,128)S(1)}, u32[]{:S(2)}, u32[]{:S(2)}) collective-permute-start(f32[2,1152]{1,0:T(2,128)S(1)} %copy.20), channel_id=1, source_target_pairs={{0,32},{32,64},{64,96},{96,128},{128,160},{160,192},{192,224},{224... | collective-permute-start | bytes 27656 | tf_op jit(solution)/shard_map/while/body/eval_jaxpr/ppermute | solution.py:12
  295.5 11.6 %collective-permute-start = (f32[2,1152]{1,0:T(2,128)S(1)}, f32[2,1152]{1,0:T(2,128)S(1)}, u32[]{:S(2)}, u32[]{:S(2)}) collective-permute-start(f32[2,1152]{1,0:T(2,128)S(1)} %copy.20), channel_id=1, source_target_pairs={{0,32},{32,64},{64,96},{96,128},{128,160},{160,192},{192,224},{224... | collective-permute-start | bytes 27656 | tf_op jit(solution)/shard_map/while/body/eval_jaxpr/ppermute | solution.py:12
  307.2 12.2 %collective-permute-start = (f32[2,1152]{1,0:T(2,128)S(1)}, f32[2,1152]{1,0:T(2,128)S(1)}, u32[]{:S(2)}, u32[]{:S(2)}) collective-permute-start(f32[2,1152]{1,0:T(2,128)S(1)} %copy.20), channel_id=1, source_target_pairs={{0,32},{32,64},{64,96},{96,128},{128,160},{160,192},{192,224},{224... | collective-permute-start | bytes 27656 | tf_op jit(solution)/shard_map/while/body/eval_jaxpr/ppermute | solution.py:12
  319.4 13.1 %collective-permute-start = (f32[2,1152]{1,0:T(2,128)S(1)}, f32[2,1152]{1,0:T(2,128)S(1)}, u32[]{:S(2)}, u32[]{:S(2)}) collective-permute-start(f32[2,1152]{1,0:T(2,128)S(1)} %copy.20), channel_id=1, source_target_pairs={{0,32},{32,64},{64,96},{96,128},{128,160},{160,192},{192,224},{224... | collective-permute-start | bytes 27656 | tf_op jit(solution)/shard_map/while/body/eval_jaxpr/ppermute | solution.py:12
  332.5 11.2 %collective-permute-start = (f32[2,1152]{1,0:T(2,128)S(1)}, f32[2,1152]{1,0:T(2,128)S(1)}, u32[]{:S(2)}, u32[]{:S(2)}) collective-permute-start(f32[2,1152]{1,0:T(2,128)S(1)} %copy.20), channel_id=1, source_target_pairs={{0,32},{32,64},{64,96},{96,128},{128,160},{160,192},{192,224},{224... | collective-permute-start | bytes 27656 | tf_op jit(solution)/shard_map/while/body/eval_jaxpr/ppermute | solution.py:12
  343.7 11.1 %collective-permute-start = (f32[2,1152]{1,0:T(2,128)S(1)}, f32[2,1152]{1,0:T(2,128)S(1)}, u32[]{:S(2)}, u32[]{:S(2)}) collective-permute-start(f32[2,1152]{1,0:T(2,128)S(1)} %copy.20), channel_id=1, source_target_pairs={{0,32},{32,64},{64,96},{96,128},{128,160},{160,192},{192,224},{224... | collective-permute-start | bytes 27656 | tf_op jit(solution)/shard_map/while/body/eval_jaxpr/ppermute | solution.py:12
  354.8 11.1 %collective-permute-start = (f32[2,1152]{1,0:T(2,128)S(1)}, f32[2,1152]{1,0:T(2,128)S(1)}, u32[]{:S(2)}, u32[]{:S(2)}) collective-permute-start(f32[2,1152]{1,0:T(2,128)S(1)} %copy.20), channel_id=1, source_target_pairs={{0,32},{32,64},{64,96},{96,128},{128,160},{160,192},{192,224},{224... | collective-permute-start | bytes 27656 | tf_op jit(solution)/shard_map/while/body/eval_jaxpr/ppermute | solution.py:12
  365.8 11.1 %collective-permute-start = (f32[2,1152]{1,0:T(2,128)S(1)}, f32[2,1152]{1,0:T(2,128)S(1)}, u32[]{:S(2)}, u32[]{:S(2)}) collective-permute-start(f32[2,1152]{1,0:T(2,128)S(1)} %copy.20), channel_id=1, source_target_pairs={{0,32},{32,64},{64,96},{96,128},{128,160},{160,192},{192,224},{224... | collective-permute-start | bytes 27656 | tf_op jit(solution)/shard_map/while/body/eval_jaxpr/ppermute | solution.py:12
  376.9 11.1 %collective-permute-start = (f32[2,1152]{1,0:T(2,128)S(1)}, f32[2,1152]{1,0:T(2,128)S(1)}, u32[]{:S(2)}, u32[]{:S(2)}) collective-permute-start(f32[2,1152]{1,0:T(2,128)S(1)} %copy.20), channel_id=1, source_target_pairs={{0,32},{32,64},{64,96},{96,128},{128,160},{160,192},{192,224},{224... | collective-permute-start | bytes 27656 | tf_op jit(solution)/shard_map/while/body/eval_jaxpr/ppermute | solution.py:12
  388.0 11.1 %collective-permute-start = (f32[2,1152]{1,0:T(2,128)S(1)}, f32[2,1152]{1,0:T(2,128)S(1)}, u32[]{:S(2)}, u32[]{:S(2)}) collective-permute-start(f32[2,1152]{1,0:T(2,128)S(1)} %copy.20), channel_id=1, source_target_pairs={{0,32},{32,64},{64,96},{96,128},{128,160},{160,192},{192,224},{224... | collective-permute-start | bytes 27656 | tf_op jit(solution)/shard_map/while/body/eval_jaxpr/ppermute | solution.py:12
  391.1 8.0 collective-permute-start.1
  399.1 11.1 %collective-permute-start = (f32[2,1152]{1,0:T(2,128)S(1)}, f32[2,1152]{1,0:T(2,128)S(1)}, u32[]{:S(2)}, u32[]{:S(2)}) collective-permute-start(f32[2,1152]{1,0:T(2,128)S(1)} %copy.20), channel_id=1, source_target_pairs={{0,32},{32,64},{64,96},{96,128},{128,160},{160,192},{192,224},{224... | collective-permute-start | bytes 27656 | tf_op jit(solution)/shard_map/while/body/eval_jaxpr/ppermute | solution.py:12
  421.3 355.5 %all-reduce.54.cloned.1.call-start = ((), (), s32[]{:S(2)}) async-start(), calls=%async_computation.4 | async-start | bytes 344064 | tf_op jit(solution)/shard_map/psum | solution.py:115
  440.2 488.0 %all-reduce.58.cloned.1.call-start = ((), (), s32[]{:S(2)}) async-start(), calls=%async_computation.7 | async-start | bytes 147456 | tf_op jit(solution)/shard_map/psum | solution.py:119
  559.3 531.5 %all-reduce.56.cloned.1.call-start = ((), (), s32[]{:S(2)}) async-start(), calls=%async_computation.5 | async-start | bytes 344064 | tf_op jit(solution)/shard_map/psum | solution.py:115
  (22 other events, 399.2 us)
Sparse Core Ops, SparseCore 0:
  10.1 74.2 all-gather.3
  86.5 67.7 all-gather.5
  156.5 66.9 all-gather.7
  421.4 137.7 reduce-scatter.1
  562.6 214.1 all-reduce.53
  779.8 148.3 all-reduce.57
  931.1 159.5 all-reduce.55
